TPU v7x, 32 devices: a whole 2x2x4 slice. The times are simulated.
32 devices in a mesh: tm: 8 (over y, x, core), row: 4 (over z).
Axes of the slice: x: 2, y: 2, z: 4, core: 2. Of those that a mesh axis runs over, the one named last changes fastest.
Arguments:
- frames_in: bfloat16 [32, 16, 64, 512], P('tm', 'row'), may hold values from -6 to 6
- state_in: float32 [16, 64, 512], P('row'), may hold values from -12 to 12
- modulus: float32 [32, 256], replicated, may hold values from 0.05 to 1
- angle: float32 [256], replicated, may hold values from -3.140625 to 3.140625
- w_in: bfloat16 [3, 3, 512, 512], replicated, may hold values from -0.09375 to 0.09375
- w_out: bfloat16 [3, 3, 512, 512], replicated, may hold values from -0.0234375 to 0.0234375
Outputs:
- output: bfloat16 [32, 16, 64, 512], P('tm', 'row')
All inputs are finite; a program needn't handle non-finite values.
Results may differ from a plain program's by a relative error of at most 0.005.
Values may be sent and summed in bfloat16 or wider, within the bound.
A program may use at most 64 MiB of HBM per device.

v0:
```python
import jax
import jax.numpy as jnp
from jax import lax
from jax.sharding import PartitionSpec as P


def with_halo(block, sides, width):
    for axis, dim in sides:
        count = lax.axis_size(axis)
        forward = [(i, i + 1) for i in range(count - 1)]
        backward = [(target, source) for source, target in forward]
        low = lax.ppermute(
            lax.slice_in_dim(block, block.shape[dim] - width, None, axis=dim), axis, forward
        )
        high = lax.ppermute(lax.slice_in_dim(block, 0, width, axis=dim), axis, backward)
        block = jnp.concatenate([low, block, high], axis=dim)
    return block


def prefix(part, axis, combine, identity):
    place = lax.axis_index(axis)
    gathered = jax.tree.map(lambda a: lax.all_gather(a, axis), part)
    state = jax.tree.map(lambda a, e: jnp.zeros_like(a) + jnp.asarray(e, a.dtype), part, identity)

    def one(hop, state):
        return combine(
            state, jax.tree.map(lambda a: lax.dynamic_index_in_dim(a, hop, 0, False), gathered)
        )

    return lax.fori_loop(0, place, one, state)


def conv_rows(padded, weight):
    count_frames, rows_in, columns, channels = padded.shape
    rows_out = rows_in - 2
    outputs = weight.shape[3]
    widened = jnp.pad(padded, ((0, 0), (0, 0), (1, 1), (0, 0)))
    summed = jnp.zeros((count_frames * rows_out * columns, outputs), jnp.float32)
    for row_tap in range(3):
        for col_tap in range(3):
            window = widened[
                :, row_tap : row_tap + rows_out, col_tap : col_tap + columns, :
            ].reshape(count_frames * rows_out * columns, channels)
            summed = summed + jnp.dot(
                window, weight[row_tap, col_tap], preferred_element_type=jnp.float32
            )
    return summed.reshape(count_frames, rows_out, columns, outputs)


def convolve(padded, weight):
    return conv_rows(padded, weight)


def rotate(rate_re, rate_im, values):
    half = values.shape[-1] // 2
    part_re = values[..., :half]
    part_im = values[..., half:]
    return jnp.concatenate(
        [rate_re * part_re - rate_im * part_im, rate_im * part_re + rate_re * part_im], axis=-1
    )


def complex_mul(left_re, left_im, right_re, right_im):
    return (left_re * right_re - left_im * right_im, left_re * right_im + left_im * right_re)


def shards(frames_in, state_in, modulus, angle, w_in, w_out):
    count_frames = frames_in.shape[0]
    padded = with_halo(frames_in, (("row", 1),), 1)
    driven = convolve(padded, w_in)
    cos_part = jnp.cos(angle)
    sin_part = jnp.sin(angle)
    offset_frame = lax.axis_index("tm") * count_frames
    local_mod = lax.dynamic_slice_in_dim(modulus, offset_frame, count_frames, 0)
    rate_re = local_mod * cos_part[None, :]
    rate_im = local_mod * sin_part[None, :]
    running = driven[0]
    prod_re = rate_re[0]
    prod_im = rate_im[0]
    locals_list = [running]
    products = [(prod_re, prod_im)]
    for frame_index in range(1, count_frames):
        running = rotate(rate_re[frame_index], rate_im[frame_index], running) + driven[frame_index]
        prod_re, prod_im = complex_mul(rate_re[frame_index], rate_im[frame_index], prod_re, prod_im)
        locals_list.append(running)
        products.append((prod_re, prod_im))

    def combine(earlier, latter):
        early_rate, early_state = earlier
        late_rate, late_state = latter
        new_re, new_im = complex_mul(late_rate[0], late_rate[1], early_rate[0], early_rate[1])
        joined = rotate(late_rate[0], late_rate[1], early_state) + late_state
        return (jnp.stack([new_re, new_im]), joined)

    identity = (
        jnp.stack([jnp.ones_like(prod_re), jnp.zeros_like(prod_re)]),
        jnp.zeros_like(running),
    )
    prefix_rate, prefix_state = prefix(
        (jnp.stack([prod_re, prod_im]), running), "tm", combine, identity
    )
    incoming = rotate(prefix_rate[0], prefix_rate[1], state_in) + prefix_state
    states_all = [
        locals_list[frame_index]
        + rotate(products[frame_index][0], products[frame_index][1], incoming)
        for frame_index in range(count_frames)
    ]
    states_bf = jnp.stack(states_all).astype(jnp.bfloat16)
    padded_state = with_halo(states_bf, (("row", 1),), 1)
    return jax.nn.gelu(convolve(padded_state, w_out), approximate=False).astype(jnp.bfloat16)


def solution(mesh):
    return jax.shard_map(
        shards,
        mesh=mesh,
        in_specs=(P("tm", "row", None, None), P("row", None, None), P(), P(), P(), P()),
        out_specs=P("tm", "row", None, None),
        check_vma=False,
    )
```

profile of v0, /device:TPU:7, one launch (start us, length us, event | category | flops | bytes accessed | tf_op | source)
XLA Modules:
  0.0 113.9 jit_solution(13187284045210578954)
XLA Ops:
  6.5 1.1 fusion.92
  7.6 3.3 %collective-permute-start = (bf16[4,1,64,512]{3,2,1,0:T(8,128)(2,1)S(1)}, bf16[4,1,64,512]{3,2,1,0:T(8,128)(2,1)S(1)}, u32[]{:S(2)}, u32[]{:S(2)}) collective-permute-start(bf16[4,1,64,512]{3,2,1,0:T(8,128)(2,1)S(1)} %get-tuple-element.90), channel_id=1, source_target_pairs={{0,1},{1,2},{2,3},{4,5},{5,6},{6,7},{8,9},{9,10},{10,11},{12,13},{... | collective-permute-start | bytes 786440 | tf_op jit(solution)/shard_map/ppermute | solution.py:12
  11.0 1.3 %collective-permute-start.1 = (bf16[4,1,64,512]{3,2,1,0:T(8,128)(2,1)S(1)}, bf16[4,1,64,512]{3,2,1,0:T(8,128)(2,1)S(1)}, u32[]{:S(2)}, u32[]{:S(2)}) collective-permute-start(bf16[4,1,64,512]{3,2,1,0:T(8,128)(2,1)S(1)} %get-tuple-element.91), channel_id=1, source_target_pairs={{1,0},{2,1},{3,2},{5,4},{6,5},{7,6},{9,8},{10,9},{11,10},{13,12},{... | collective-permute-start | bytes 786440 | tf_op jit(solution)/shard_map/ppermute | solution.py:15
  12.3 0.7 fusion.95
  13.0 0.7 dynamic-slice_multiply_fusion.1
  13.7 2.1 %fusion.60 = f32[1024,512]{1,0:T(8,128)S(1)} fusion(bf16[1024,512]{1,0:T(8,128)(2,1)} %bitcast.173, bf16[3,3,512,512]{3,2,1,0:T(8,128)(2,1)} %param.12), kind=kOutput, calls=%fused_computation.101 | convolution fusion | flops 536870912 | bytes 3670016 | tf_op jit(solution)/shard_map/dot_general | solution.py:44
  15.8 0.1 collective-permute-done
  15.9 3.8 %collective-permute-done.1 = bf16[4,1,64,512]{3,2,1,0:T(8,128)(2,1)S(1)} collective-permute-done((bf16[4,1,64,512]{3,2,1,0:T(8,128)(2,1)S(1)}, bf16[4,1,64,512]{3,2,1,0:T(8,128)(2,1)S(1)}, u32[]{:S(2)}, u32[]{:S(2)}) %collective-permute-start.1) | collective-permute-done | bytes 262176 | tf_op jit(solution)/shard_map/ppermute | solution.py:15
  19.7 0.9 fusion.20
  20.7 1.3 %fusion.90 = (bf16[4,4,64,512]{3,2,1,0:T(8,128)(2,1)S(1)}, bf16[4,4,64,512]{3,2,1,0:T(8,128)(2,1)S(1)}, bf16[4,4,64,512]{3,2,1,0:T(8,128)(2,1)S(1)}, bf16[4,4,64...) fusion(bf16[4,6,66,512]{3,2,1,0:T(8,128)(2,1)S(1)} %fusion.20), kind=kLoop, calls=%fused_computation.162 | loop fusion | bytes 12582912 | tf_op jit(solution)/shard_map/slice | solution.py:41
  22.0 0.2 slice-done.1
  22.3 0.7 fusion.56
  23.0 0.7 fusion.58
  23.7 0.7 fusion.62
  24.4 0.7 fusion.64
  25.1 0.7 fusion.68
  25.8 0.2 pad_maximum_fusion.10
  26.0 0.7 fusion.54
  26.7 0.7 fusion.66
  27.4 1.5 %add_add_fusion.1 = f32[1024,512]{1,0:T(8,128)S(1)} fusion(f32[1024,512]{1,0:T(8,128)S(1)} %fusion.54, f32[1024,512]{1,0:T(8,128)S(1)} %fusion.56, f32[1024,512]{1,0:T(8,128)S(1)} %fusion.58, f32[1024,512]{1,0:T(8,128)S(1)} %fusion.60, f32[1024,512]{1,0:T(8,128)S(1)} %fusion.62, f32[1024,512]{1,0:T(8,128)S(1)} %fusion.64, f32[1024,512]{1,0:T(8,128)S(1)} %fusion.68, ...), kind=kOutput, calls=%fused_computation.33 | convolution fusion | flops 541065216 | bytes 20447232 | tf_op jit(solution)/shard_map/dot_general | solution.py:44
  28.9 0.2 fusion.88
  29.1 0.1 multiply_subtract_fusion.3
  29.1 0.1 maximum_add_fusion.1
  29.2 0.1 multiply_subtract_fusion.2
  29.3 0.1 maximum_add_fusion.2
  29.4 0.1 subtract_bitcast_fusion.4
  29.4 0.9 maximum_add_fusion.3
  30.4 9.6 %all-gather.1 = f32[8,2,256]{2,1,0:T(2,128)S(1)} all-gather(f32[1,2,256]{2,1,0:T(2,128)S(1)} %maximum_bitcast_fusion), channel_id=2, replica_groups=mesh['tm'=8,'row'=4] {'tm'}, dimensions={0}, use_global_device_ids=true | all-gather | bytes 18432 | tf_op jit(solution)/shard_map/all_gather | solution.py:22
  40.0 28.1 %all-gather.4.cloned.1.call-done = f32[8,4,64,512]{3,2,1,0:T(8,128)} async-done(((f32[1,4,64,512]{3,2,1,0:T(8,128)}), f32[8,4,64,512]{3,2,1,0:T(8,128)}) %all-gather.4.cloned.1.call-update) | async-done | bytes 4194320 | tf_op jit(solution)/shard_map/all_gather | solution.py:22
  68.1 8.8 %while.12 = (s32[]{:T(128)}, f32[2,256]{1,0:T(2,128)S(1)}, f32[4,64,512]{2,1,0:T(8,128)S(1)}, s32[]{:T(128)}, f32[8,2,256]{2,1,0:T(2,128)S(1)}, /*index=5*/f32[8...) while((s32[]{:T(128)}, f32[2,256]{1,0:T(2,128)S(1)}, f32[4,64,512]{2,1,0:T(8,128)S(1)}, ...), condition=%wide.region_1.2_spmd, body=%wide.region_0.1_spmd.sunk | while | flops 657414 | bytes 2640031 | solution.py:30
  68.2 0.1 multiply_subtract_fusion.14
  68.3 1.1 maximum_add_fusion.10
  69.5 1.1 maximum_add_fusion.10
  70.7 0.1 multiply_subtract_fusion.14
  70.8 1.1 maximum_add_fusion.10
  72.0 1.1 maximum_add_fusion.10
  73.3 1.1 maximum_add_fusion.10
  74.5 1.1 maximum_add_fusion.10
  75.8 1.1 maximum_add_fusion.10
  77.0 1.1 multiply_subtract_fusion.1
  78.1 0.1 maximum_add_fusion.4
  78.2 0.2 subtract_bitcast_fusion.3
  78.4 0.1 subtract_bitcast_fusion
  78.4 0.7 copy-done.1
  79.1 0.3 fusion.28
  79.4 0.2 fusion.24
  79.6 0.1 pad_maximum_fusion.11
  79.8 3.1 %collective-permute-start.2 = (bf16[4,1,64,512]{3,2,1,0:T(8,128)(2,1)S(1)}, bf16[4,1,64,512]{3,2,1,0:T(8,128)(2,1)S(1)}, u32[]{:S(2)}, u32[]{:S(2)}) collective-permute-start(bf16[4,1,64,512]{3,2,1,0:T(8,128)(2,1)S(1)} %get-tuple-element.86), channel_id=1, source_target_pairs={{0,1},{1,2},{2,3},{4,5},{5,6},{6,7},{8,9},{9,10},{10,11},{12,13},{... | collective-permute-start | bytes 786440 | tf_op jit(solution)/shard_map/ppermute | solution.py:12
  83.0 1.5 %collective-permute-start.3 = (bf16[4,1,64,512]{3,2,1,0:T(8,128)(2,1)S(1)}, bf16[4,1,64,512]{3,2,1,0:T(8,128)(2,1)S(1)}, u32[]{:S(2)}, u32[]{:S(2)}) collective-permute-start(bf16[4,1,64,512]{3,2,1,0:T(8,128)(2,1)S(1)} %get-tuple-element.87), channel_id=1, source_target_pairs={{1,0},{2,1},{3,2},{5,4},{6,5},{7,6},{9,8},{10,9},{11,10},{13,12},{... | collective-permute-start | bytes 786440 | tf_op jit(solution)/shard_map/ppermute | solution.py:15
  84.5 0.7 fusion.40
  85.2 3.3 %collective-permute-done.2 = bf16[4,1,64,512]{3,2,1,0:T(8,128)(2,1)S(1)} collective-permute-done((bf16[4,1,64,512]{3,2,1,0:T(8,128)(2,1)S(1)}, bf16[4,1,64,512]{3,2,1,0:T(8,128)(2,1)S(1)}, u32[]{:S(2)}, u32[]{:S(2)}) %collective-permute-start.2) | collective-permute-done | bytes 262176 | tf_op jit(solution)/shard_map/ppermute | solution.py:12
  88.5 4.1 %collective-permute-done.3 = bf16[4,1,64,512]{3,2,1,0:T(8,128)(2,1)S(1)} collective-permute-done((bf16[4,1,64,512]{3,2,1,0:T(8,128)(2,1)S(1)}, bf16[4,1,64,512]{3,2,1,0:T(8,128)(2,1)S(1)}, u32[]{:S(2)}, u32[]{:S(2)}) %collective-permute-start.3) | collective-permute-done | bytes 262176 | tf_op jit(solution)/shard_map/ppermute | solution.py:15
  92.6 0.3 pad_maximum_fusion.5
  92.9 0.7 fusion.34
  93.6 0.7 fusion.46
  94.4 1.1 select_maximum_fusion
  95.4 1.3 %fusion.89 = (bf16[4,4,64,512]{3,2,1,0:T(8,128)(2,1)S(1)}, bf16[4,4,64,512]{3,2,1,0:T(8,128)(2,1)S(1)}, bf16[4,4,64,512]{3,2,1,0:T(8,128)(2,1)S(1)}, bf16[4,4,64...) fusion(bf16[4,6,66,512]{3,2,1,0:T(8,128)(2,1)S(1)} %select_maximum_fusion), kind=kLoop, calls=%fused_computation.161 | loop fusion | bytes 12582912 | tf_op jit(solution)/shard_map/slice | solution.py:41
  96.8 0.7 fusion.36
  97.5 0.7 fusion.38
  98.2 0.7 fusion.42
  98.9 0.7 fusion.44
  99.6 0.7 fusion.48
  100.3 1.6 %negate_multiply_fusion = (f32[1024,512]{1,0:T(8,128)S(1)}, f32[1024,512]{1,0:T(8,128)S(1)}) fusion(bf16[1024,512]{1,0:T(8,128)(2,1)S(1)} %bitcast.188, bf16[3,3,512,512]{3,2,1,0:T(8,128)(2,1)S(1)} %bitcast.180, f32[1024,512]{1,0:T(8,128)S(1)} %fusion.34, f32[1024,512]{1,0:T(8,128)S(1)} %fusion.36, f32[1024,512]{1,0:T(8,128)S(1)} %fusion.38, ...), kind=kOutput, calls=%fused_computation.31 | convolution fusion | flops 542638080 | bytes 22544384 | tf_op jit(solution)/shard_map/dot_general | solution.py:44
  101.9 5.2 %fusion.5 = bf16[4,4,64,512]{3,2,1,0:T(8,128)(2,1)} fusion(f32[4,4,64,512]{3,2,1,0:T(8,128)S(1)} %bitcast.175, f32[4,4,64,512]{3,2,1,0:T(8,128)S(1)} %bitcast.174), kind=kLoop, calls=%fused_computation.18 | loop fusion | flops 32505856 | bytes 5242880 | tf_op jit(solution)/shard_map/convert_element_type | solution.py:110
  (51 shorter events, 0.7 us)
Async XLA Ops:
  6.5 61.5 %all-gather.4.cloned.1.call-start = ((), (), s32[]{:S(2)}) async-start(), calls=%async_computation | async-start | bytes 4718592 | tf_op jit(solution)/shard_map/all_gather | solution.py:22
  7.6 12.1 %copy-start = (bf16[4,4,64,512]{3,2,1,0:T(8,128)(2,1)S(1)}, bf16[4,4,64,512]{3,2,1,0:T(8,128)(2,1)}, u32[]{:S(2)}) copy-start(bf16[4,4,64,512]{3,2,1,0:T(8,128)(2,1)} %param.8) | copy-start | bytes 3145732
  7.6 8.3 %collective-permute-start = (bf16[4,1,64,512]{3,2,1,0:T(8,128)(2,1)S(1)}, bf16[4,1,64,512]{3,2,1,0:T(8,128)(2,1)S(1)}, u32[]{:S(2)}, u32[]{:S(2)}) collective-permute-start(bf16[4,1,64,512]{3,2,1,0:T(8,128)(2,1)S(1)} %get-tuple-element.90), channel_id=1, source_target_pairs={{0,1},{1,2},{2,3},{4,5},{5,6},{6,7},{8,9},{9,10},{10,11},{12,13},{... | collective-permute-start | bytes 786440 | tf_op jit(solution)/shard_map/ppermute | solution.py:12
  11.0 8.8 %collective-permute-start.1 = (bf16[4,1,64,512]{3,2,1,0:T(8,128)(2,1)S(1)}, bf16[4,1,64,512]{3,2,1,0:T(8,128)(2,1)S(1)}, u32[]{:S(2)}, u32[]{:S(2)}) collective-permute-start(bf16[4,1,64,512]{3,2,1,0:T(8,128)(2,1)S(1)} %get-tuple-element.91), channel_id=1, source_target_pairs={{1,0},{2,1},{3,2},{5,4},{6,5},{7,6},{9,8},{10,9},{11,10},{13,12},{... | collective-permute-start | bytes 786440 | tf_op jit(solution)/shard_map/ppermute | solution.py:15
  19.7 2.3 %slice-start = ((s8[4718592]{0:T(1024)(128)(4,1)}), s8[4194304]{0:T(1024)(128)(4,1)S(1)}, s32[]{:S(2)}) async-start(s8[4718592]{0:T(1024)(128)(4,1)} %bitcast.177), calls=%async_computation.1 | async-start | bytes 8388608
  20.7 1.6 %slice-start.1 = ((s8[4718592]{0:T(1024)(128)(4,1)}), s8[524288]{0:T(1024)(128)(4,1)S(1)}, s32[]{:S(2)}) async-start(s8[4718592]{0:T(1024)(128)(4,1)} %bitcast.177), calls=%async_computation.2 | async-start | bytes 1048576
  29.4 38.8 %copy-start.2 = (f32[2,256]{1,0:T(2,128)S(1)}, f32[2,256]{1,0:T(2,128)}, u32[]{:S(2)}) copy-start(f32[2,256]{1,0:T(2,128)} %constant.15.clone.1) | copy-start | bytes 6148
  78.1 1.0 copy-start.1
  78.1 6.4 %slice-start.2 = ((s8[4718592]{0:T(1024)(128)(4,1)}), s8[4194304]{0:T(1024)(128)(4,1)S(1)}, s32[]{:S(2)}) async-start(s8[4718592]{0:T(1024)(128)(4,1)} %bitcast.179), calls=%async_computation.3 | async-start | bytes 8388608
  79.1 5.3 %slice-start.3 = ((s8[4718592]{0:T(1024)(128)(4,1)}), s8[524288]{0:T(1024)(128)(4,1)S(1)}, s32[]{:S(2)}) async-start(s8[4718592]{0:T(1024)(128)(4,1)} %bitcast.179), calls=%async_computation.4 | async-start | bytes 1048576
  79.8 8.7 %collective-permute-start.2 = (bf16[4,1,64,512]{3,2,1,0:T(8,128)(2,1)S(1)}, bf16[4,1,64,512]{3,2,1,0:T(8,128)(2,1)S(1)}, u32[]{:S(2)}, u32[]{:S(2)}) collective-permute-start(bf16[4,1,64,512]{3,2,1,0:T(8,128)(2,1)S(1)} %get-tuple-element.86), channel_id=1, source_target_pairs={{0,1},{1,2},{2,3},{4,5},{5,6},{6,7},{8,9},{9,10},{10,11},{12,13},{... | collective-permute-start | bytes 786440 | tf_op jit(solution)/shard_map/ppermute | solution.py:12
  83.0 9.7 %collective-permute-start.3 = (bf16[4,1,64,512]{3,2,1,0:T(8,128)(2,1)S(1)}, bf16[4,1,64,512]{3,2,1,0:T(8,128)(2,1)S(1)}, u32[]{:S(2)}, u32[]{:S(2)}) collective-permute-start(bf16[4,1,64,512]{3,2,1,0:T(8,128)(2,1)S(1)} %get-tuple-element.87), channel_id=1, source_target_pairs={{1,0},{2,1},{3,2},{5,4},{6,5},{7,6},{9,8},{10,9},{11,10},{13,12},{... | collective-permute-start | bytes 786440 | tf_op jit(solution)/shard_map/ppermute | solution.py:15
Sparse Core Ops, SparseCore 0:
  30.5 37.5 all-gather.3
where the time goes:
time: 115 us; the launch traced here: 114 us
  waiting for transfers between devices  39.5 us (34%)
  other arithmetic  20 us (17%)
  matrix products  15.7 us (14%)
  between operations  13.8 us (12%)
  blocking collectives  9.6 us (8%)
  starting transfers between devices  9.24 us (8%)
  local copies, waits for them, and re-layouts  5.67 us (5%)
    all_gather x1, waiting for transfers between devices, prefix(): gathered = jax.tree.map(lambda a: lax.all_gather(a, axis), part)  28.1 us
    dot_general x18, matrix products, conv_rows(): jnp.dot(window, weight[row_tap, col_tap], preferred_element_type=jnp.floa...  15.7 us
    all_gather x1, blocking collectives, prefix(): gathered = jax.tree.map(lambda a: lax.all_gather(a, axis), part)  9.6 us
    ppermute x2, waiting for transfers between devices, with_halo(): lax.ppermute(lax.slice_in_dim(block, 0, width, axis=dim), axis, backward)  7.95 us
    add x7, other arithmetic, combine(): joined = rotate(late_rate[0], late_rate[1], early_state) + late_state  7.79 us
    ppermute x2, starting transfers between devices, with_halo(): lax.ppermute(lax.slice_in_dim(block, block.shape[dim] - width, None, axis...  6.47 us
    convert_element_type x1, other arithmetic, shards(): jax.nn.gelu(convolve(padded_state, w_out), approximate=False)  5.15 us
    ppermute x2, waiting for transfers between devices, with_halo(): lax.ppermute(lax.slice_in_dim(block, block.shape[dim] - width, None, axis...  3.42 us
  transfers between devices with their start and end apart: 5, of which 5 were waited for; matrix products, arithmetic and copies ran while one was open for 4% of the time, Pallas kernels for 0%

commit v1 on v0

v1 whole, which is shorter than its diff:
```python
import functools

import jax
import jax.numpy as jnp
from jax import lax
from jax.experimental import pallas as pl
from jax.experimental.pallas import tpu as pltpu
from jax.sharding import PartitionSpec as P

MESH = pl.DeviceIdType.MESH
F32 = jnp.float32
BF16 = jnp.bfloat16


def gelu(v):
    return v * (0.5 + 0.5 * lax.erf(v * 0.7071067811865476))


def rot(re, im, v):
    half = v.shape[-1] // 2
    p, q = v[:, :half], v[:, half:]
    return jnp.concatenate([re * p - im * q, im * p + re * q], axis=-1)


def kernel(
    n_tm, n_row, steps,
    frames_hbm, state_hbm, mod_ref, ang_ref, win_hbm, wout_hbm, out_ref,
    frames_v, state_v, win, wout, x1, x2, acc, loc, tab_re, tab_im,
    t_buf, r_buf, s_send, s_recv, fh_recv, lh_send, lh_recv, ih_send, ih_recv,
    load_sem, s_ssem, s_rsem, fh_ssem, fh_rsem, lh_ssem, lh_rsem, ih_ssem, ih_rsem,
):
    F, R, W, C = frames_hbm.shape
    half = C // 2
    FW = F * W
    K3 = 3 * C
    me = lax.axis_index("tm")
    row = lax.axis_index("row")
    has_up, has_down = row > 0, row < n_row - 1
    sides = ((has_up, row - 1), (has_down, row + 1))
    partners = [me + (1 - 2 * ((me >> k) & 1)) * (1 << k) for k in range(steps)]

    ld_frames = pltpu.make_async_copy(frames_hbm, frames_v, load_sem.at[0])
    ld_frames.start()
    ld_win = pltpu.make_async_copy(win_hbm, win, load_sem.at[1])
    ld_win.start()
    ld_state = pltpu.make_async_copy(state_hbm, state_v, load_sem.at[2])
    ld_state.start()
    ld_wout = pltpu.make_async_copy(wout_hbm, wout, load_sem.at[3])

    barrier = pltpu.get_barrier_semaphore()
    for p in partners:
        pl.semaphore_signal(barrier, inc=1, device_id={"tm": p}, device_id_type=MESH)
    for has, where in sides:
        @pl.when(has)
        def _():
            pl.semaphore_signal(barrier, inc=1, device_id={"row": where}, device_id_type=MESH)
    pl.semaphore_wait(barrier, steps + has_up.astype(jnp.int32) + has_down.astype(jnp.int32))

    def remote(src, dst, ssem, rsem, dev):
        return pltpu.make_async_remote_copy(
            src_ref=src, dst_ref=dst, send_sem=ssem, recv_sem=rsem,
            device_id=dev, device_id_type=MESH,
        )

    edge = (0, R - 1)
    fh = [
        remote(frames_hbm.at[:, edge[s]], fh_recv.at[1 - s], fh_ssem.at[s], fh_rsem.at[1 - s],
               {"row": sides[s][1]})
        for s in range(2)
    ]
    fh_in = [
        remote(frames_hbm.at[:, edge[s]], fh_recv.at[s], fh_ssem.at[s], fh_rsem.at[s],
               {"row": sides[s][1]})
        for s in range(2)
    ]
    for s in range(2):
        @pl.when(sides[s][0])
        def _():
            fh[s].start()

    rows = tab_re.shape[0]
    idx = lax.broadcasted_iota(jnp.int32, (rows, 1), 0)
    lo = jnp.zeros((rows, 1), jnp.int32)
    hi = jnp.zeros((rows, 1), jnp.int32)
    keep = jnp.ones((rows, 1), jnp.int32)
    for t in range(F):
        lo = jnp.where(idx == t, me * F + t, lo)
        hi = jnp.where(idx == t, me * F + t + 1, hi)
        lo = jnp.where(idx == F + t, me * F, lo)
        hi = jnp.where(idx == F + t, me * F + t + 1, hi)
    ups = []
    for k in range(steps):
        size = 1 << k
        up = (me >> k) & 1
        ups.append(up)
        base = (me >> k) << k
        top = ((me >> k) | 1) << k
        i_a, i_b = 2 * F + k, 2 * F + steps + k
        lo = jnp.where(idx == i_a, top * F, lo)
        hi = jnp.where(idx == i_a, (top + size) * F, hi)
        lo = jnp.where(idx == i_b, base * F, lo)
        hi = jnp.where(idx == i_b, me * F, hi)
        keep = jnp.where(idx == i_b, up, keep)
    mod = jnp.ones((rows, half), F32) * keep.astype(F32)
    for f in range(n_tm * F):
        mod = mod * jnp.where((lo <= f) & (f < hi), mod_ref[f:f + 1, :], 1.0)
    phase = (hi - lo).astype(F32) * ang_ref[...]
    tab_re[...] = mod * jnp.cos(phase)
    tab_im[...] = mod * jnp.sin(phase)

    def table(i):
        return tab_re[i:i + 1, :], tab_im[i:i + 1, :]

    def spread(x, r, f0, v):
        n = v.shape[0]
        col = lax.broadcasted_iota(jnp.int32, (n, 1), 0) % W
        at = slice(f0 * W, f0 * W + n)
        x[r, at, C:2 * C] = v.astype(BF16)
        x[r, at, 0:C] = jnp.where(col == 0, 0.0, pltpu.roll(v, 1, 0)).astype(BF16)
        x[r, at, 2 * C:] = jnp.where(col == W - 1, 0.0, pltpu.roll(v, n - 1, 0)).astype(BF16)

    def taps(x, w, r0, count, a0, a1):
        m = count * FW
        lhs = jnp.concatenate(
            [x[r0 + a:r0 + a + count].reshape(m, K3) for a in range(a0, a1)], axis=-1
        )
        return jnp.dot(lhs, w[a0 * K3:a1 * K3, :], preferred_element_type=F32).reshape(count, FW, C)

    order = list(range(1, R - 1)) + [0, R - 1]
    groups = ((0, R - 2), (R - 2, R))
    first = (me == 0).astype(F32)

    def local_scan(g):
        for pos in range(*groups[g]):
            r = order[pos]
            run = state_v[r] * first
            for t in range(F):
                run = rot(*table(t), run) + acc[r, t * W:(t + 1) * W]
                loc[r, t * W:(t + 1) * W] = run
            t_buf[pos] = run
            s_send[0, pos] = run.astype(BF16)
            r_buf[pos] = jnp.zeros_like(run)

    def hop(k, g):
        at = pl.ds(groups[g][0], groups[g][1] - groups[g][0])
        return remote(s_send.at[k, at], s_recv.at[k, at], s_ssem.at[k, g], s_rsem.at[k, g],
                      {"tm": partners[k]})

    def combine(k, g):
        hop(k, g).wait_recv()
        up = ups[k] == 1
        for pos in range(*groups[g]):
            got = s_recv[k, pos].astype(F32)
            if k < steps - 1:
                mine = t_buf[pos]
                low = jnp.where(up, got, mine)
                high = jnp.where(up, mine, got)
                new = rot(*table(2 * F + k), low) + high
                t_buf[pos] = new
                s_send[k + 1, pos] = new.astype(BF16)
            r_buf[pos] = r_buf[pos] + rot(*table(2 * F + steps + k), got)
        if k < steps - 1:
            hop(k + 1, g).start()

    def states(g):
        for pos in range(*groups[g]):
            r = order[pos]
            for t in range(F):
                v = loc[r, t * W:(t + 1) * W] + rot(*table(F + t), r_buf[pos])
                spread(x2, r + 1, t, v)

    ld_frames.wait()
    for r in range(R):
        spread(x1, r + 1, 0, frames_v[:, r].reshape(FW, C).astype(F32))
    ld_win.wait()
    ld_wout.start()
    acc[1:R - 1] = taps(x1, win, 1, R - 2, 0, 3)
    ld_state.wait()
    local_scan(0)
    hop(0, 0).start()
    acc[0:1] = taps(x1, win, 0, 1, 1, 3)
    combine(0, 0)
    acc[R - 1:R] = taps(x1, win, R - 1, 1, 0, 2)
    if steps > 1:
        combine(1, 0)
    for s in range(2):
        @pl.when(sides[s][0])
        def _():
            fh_in[s].wait_recv()
            spread(x1, s * (R + 1), 0, fh_recv[s].reshape(FW, C).astype(F32))

        @pl.when(jnp.logical_not(sides[s][0]))
        def _():
            x1[s * (R + 1)] = jnp.zeros((FW, K3), BF16)
    acc[0:1] += taps(x1, win, 0, 1, 0, 1)
    acc[R - 1:R] += taps(x1, win, R - 1, 1, 2, 3)
    local_scan(1)
    hop(0, 1).start()

    lh = [
        remote(lh_send.at[s], lh_recv.at[1 - s], lh_ssem.at[s], lh_rsem.at[1 - s],
               {"row": sides[s][1]})
        for s in range(2)
    ]
    lh_in = [
        remote(lh_send.at[s], lh_recv.at[s], lh_ssem.at[s], lh_rsem.at[s], {"row": sides[s][1]})
        for s in range(2)
    ]
    ih = [
        remote(ih_send.at[s], ih_recv.at[1 - s], ih_ssem.at[s], ih_rsem.at[1 - s],
               {"row": sides[s][1]})
        for s in range(2)
    ]
    ih_in = [
        remote(ih_send.at[s], ih_recv.at[s], ih_ssem.at[s], ih_rsem.at[s], {"row": sides[s][1]})
        for s in range(2)
    ]
    for s in range(2):
        lh_send[s] = loc[edge[s]].astype(BF16)

        @pl.when(sides[s][0])
        def _():
            lh[s].start()

    for k in range(2, steps):
        combine(k, 0)
    ld_wout.wait()
    states(0)
    acc[1:2] = taps(x2, wout, 1, 1, 1, 3)
    combine(0, 1)
    acc[R - 2:R - 1] = taps(x2, wout, R - 2, 1, 0, 2)
    if steps > 1:
        combine(1, 1)
    acc[0:1] = taps(x2, wout, 0, 1, 2, 3)
    acc[R - 1:R] = taps(x2, wout, R - 1, 1, 0, 1)
    for k in range(2, steps):
        combine(k, 1)
    for s in range(2):
        ih_send[s] = r_buf[R - 2 + s].astype(BF16)

        @pl.when(sides[s][0])
        def _():
            ih[s].start()
    states(1)

    def finish(r, v):
        out_ref[:, r] = gelu(v).astype(BF16).reshape(F, W, C)

    acc[0:1] += taps(x2, wout, 0, 1, 1, 2)
    acc[R - 1:R] += taps(x2, wout, R - 1, 1, 1, 2)
    finish(1, acc[1] + taps(x2, wout, 1, 1, 0, 1)[0])
    finish(R - 2, acc[R - 2] + taps(x2, wout, R - 2, 1, 2, 3)[0])
    for s in range(2):
        @pl.when(sides[s][0])
        def _():
            lh_in[s].wait_recv()
            ih_in[s].wait_recv()
            inc = ih_recv[s].astype(F32)
            for t in range(F):
                spread(x2, s * (R + 1), t, lh_recv[s, t * W:(t + 1) * W].astype(F32)
                       + rot(*table(F + t), inc))

        @pl.when(jnp.logical_not(sides[s][0]))
        def _():
            x2[s * (R + 1)] = jnp.zeros((FW, K3), BF16)
    finish(0, acc[0] + taps(x2, wout, 0, 1, 0, 1)[0])
    finish(R - 1, acc[R - 1] + taps(x2, wout, R - 1, 1, 2, 3)[0])

    for k in range(steps):
        for g in range(2):
            hop(k, g).wait_send()
    for s in range(2):
        @pl.when(sides[s][0])
        def _():
            fh[s].wait_send()
            lh[s].wait_send()
            ih[s].wait_send()


def solution(mesh):
    n_tm, n_row = mesh.shape["tm"], mesh.shape["row"]
    steps = n_tm.bit_length() - 1
    assert n_tm == 1 << steps

    def shards(frames_in, state_in, modulus, angle, w_in, w_out):
        F, R, W, C = frames_in.shape
        assert R >= 4
        n_table = -(-(2 * F + 2 * steps) // 8) * 8
        anywhere = pl.BlockSpec(memory_space=pl.ANY)
        vmem = pl.BlockSpec(memory_space=pltpu.VMEM)
        dma = pltpu.SemaphoreType.DMA
        FW = F * W
        return pl.pallas_call(
            functools.partial(kernel, n_tm, n_row, steps),
            out_shape=jax.ShapeDtypeStruct(frames_in.shape, BF16),
            in_specs=[anywhere, anywhere, vmem, vmem, anywhere, anywhere],
            out_specs=vmem,
            scratch_shapes=[
                pltpu.VMEM((F, R, W, C), BF16),
                pltpu.VMEM((R, W, C), F32),
                pltpu.VMEM((9 * C, C), BF16),
                pltpu.VMEM((9 * C, C), BF16),
                pltpu.VMEM((R + 2, FW, 3 * C), BF16),
                pltpu.VMEM((R + 2, FW, 3 * C), BF16),
                pltpu.VMEM((R, FW, C), F32),
                pltpu.VMEM((R, FW, C), F32),
                pltpu.VMEM((n_table, C // 2), F32),
                pltpu.VMEM((n_table, C // 2), F32),
                pltpu.VMEM((R, W, C), F32),
                pltpu.VMEM((R, W, C), F32),
                pltpu.VMEM((steps, R, W, C), BF16),
                pltpu.VMEM((steps, R, W, C), BF16),
                pltpu.VMEM((2, F, W, C), BF16),
                pltpu.VMEM((2, FW, C), BF16),
                pltpu.VMEM((2, FW, C), BF16),
                pltpu.VMEM((2, W, C), BF16),
                pltpu.VMEM((2, W, C), BF16),
                dma((4,)),
                dma((steps, 2)),
                dma((steps, 2)),
                dma((2,)),
                dma((2,)),
                dma((2,)),
                dma((2,)),
                dma((2,)),
                dma((2,)),
            ],
            compiler_params=pltpu.CompilerParams(
                collective_id=0, has_side_effects=True, vmem_limit_bytes=56 * 1024 * 1024
            ),
        )(
            frames_in, state_in, modulus, angle.reshape(1, -1),
            w_in.reshape(9 * C, C), w_out.reshape(9 * C, C),
        )

    return jax.shard_map(
        shards,
        mesh=mesh,
        in_specs=(P("tm", "row", None, None), P("row", None, None), P(), P(), P(), P()),
        out_specs=P("tm", "row", None, None),
        check_vma=False,
    )
```

time: 115 us -> 36.7 us (0.32)
  the two profiles are of different devices: /device:TPU:7 before, /device:TPU:0 now
where the time goes in v1:
time: 36.7 us; the launch traced here: 36.4 us
  Pallas kernels  34.2 us (93%)
  local copies, waits for them, and re-layouts  2.29 us (6%)
    pallas_call x1, Pallas kernels, shards(): pl.pallas_call(functools.partial(kernel, n_tm, n_row, steps), out_shape=j...  34.2 us
    unnamed x1, local copies, waits for them, and re-layouts  2.29 us

profile of v1, /device:TPU:0, one launch (start us, length us, event | category | flops | bytes accessed | tf_op | source)
XLA Modules:
  0.0 36.4 jit_solution(5670637329087044378)
XLA Ops:
  0.0 34.2 %shard_map.64 = bf16[4,4,64,512]{3,2,1,0:T(8,128)(2,1)} custom-call(bf16[4,4,64,512]{3,2,1,0:T(8,128)(2,1)} %frames_hbm.1, f32[4,64,512]{2,1,0:T(8,128)} %state_hbm.1, f32[32,256]{1,0:T(8,128)} %mod_ref.1, f32[1,256]{1,0:T(1,128)} %bitcast.5, bf16[4608,512]{1,0:T(8,128)(2,1)} %bitcast.3, bf16[4608,512]{1,0:T(8,128)(2,1)} %bitcast.4), custom_call_target="tpu_custom_call" | custom-call | tf_op jit(solution)/shard_map/pallas_call | solution.py:293
  34.2 2.3 %copy.8 = bf16[4,4,64,512]{3,2,1,0:T(8,128)(2,1)} copy(bf16[4,4,64,512]{3,2,1,0:T(8,128)(2,1)} %shard_map.64) | data formatting | bytes 2097152

commit v2 on v1

--- a/solution.py
+++ b/solution.py
@@ -26,8 +26,8 @@
     n_tm, n_row, steps,
     frames_hbm, state_hbm, mod_ref, ang_ref, win_hbm, wout_hbm, out_ref,
     frames_v, state_v, win, wout, x1, x2, acc, loc, tab_re, tab_im,
-    t_buf, r_buf, s_send, s_recv, fh_recv, lh_send, lh_recv, ih_send, ih_recv,
-    load_sem, s_ssem, s_rsem, fh_ssem, fh_rsem, lh_ssem, lh_rsem, ih_ssem, ih_rsem,
+    t_buf, r_buf, s_send, s_recv, fh_recv, lh_send, lh_recv, ih_send, ih_recv, c_send, c_recv,
+    load_sem, s_ssem, s_rsem, fh_ssem, fh_rsem, lh_ssem, lh_rsem, ih_ssem, ih_rsem, c_ssem, c_rsem,
 ):
     F, R, W, C = frames_hbm.shape
     half = C // 2
@@ -37,6 +37,8 @@
     row = lax.axis_index("row")
     has_up, has_down = row > 0, row < n_row - 1
     sides = ((has_up, row - 1), (has_down, row + 1))
+    core = me & 1
+    chip = me - core
     partners = [me + (1 - 2 * ((me >> k) & 1)) * (1 << k) for k in range(steps)]
 
     ld_frames = pltpu.make_async_copy(frames_hbm, frames_v, load_sem.at[0])
@@ -53,8 +55,12 @@
     for has, where in sides:
         @pl.when(has)
         def _():
-            pl.semaphore_signal(barrier, inc=1, device_id={"row": where}, device_id_type=MESH)
-    pl.semaphore_wait(barrier, steps + has_up.astype(jnp.int32) + has_down.astype(jnp.int32))
+            for other in (me, partners[0]):
+                pl.semaphore_signal(
+                    barrier, inc=1, device_id={"tm": other, "row": where}, device_id_type=MESH
+                )
+    near = has_up.astype(jnp.int32) + has_down.astype(jnp.int32)
+    pl.semaphore_wait(barrier, steps + 2 * near)
 
     def remote(src, dst, ssem, rsem, dev):
         return pltpu.make_async_remote_copy(
@@ -93,14 +99,15 @@
         size = 1 << k
         up = (me >> k) & 1
         ups.append(up)
-        base = (me >> k) << k
+        base = (me >> k) << k if k else chip
         top = ((me >> k) | 1) << k
         i_a, i_b = 2 * F + k, 2 * F + steps + k
         lo = jnp.where(idx == i_a, top * F, lo)
         hi = jnp.where(idx == i_a, (top + size) * F, hi)
         lo = jnp.where(idx == i_b, base * F, lo)
-        hi = jnp.where(idx == i_b, me * F, hi)
-        keep = jnp.where(idx == i_b, up, keep)
+        hi = jnp.where(idx == i_b, chip * F if k else me * F, hi)
+        if k:
+            keep = jnp.where(idx == i_b, up, keep)
     mod = jnp.ones((rows, half), F32) * keep.astype(F32)
     for f in range(n_tm * F):
         mod = mod * jnp.where((lo <= f) & (f < hi), mod_ref[f:f + 1, :], 1.0)
@@ -141,15 +148,22 @@
             s_send[0, pos] = run.astype(BF16)
             r_buf[pos] = jnp.zeros_like(run)
 
+    def own(g):
+        count = (groups[g][1] - groups[g][0]) // 2
+        return groups[g][0] + core * count, count
+
     def hop(k, g):
-        at = pl.ds(groups[g][0], groups[g][1] - groups[g][0])
+        start, count = own(g)
+        at = pl.ds(start, count) if k else pl.ds(groups[g][0], 2 * count)
         return remote(s_send.at[k, at], s_recv.at[k, at], s_ssem.at[k, g], s_rsem.at[k, g],
                       {"tm": partners[k]})
 
     def combine(k, g):
         hop(k, g).wait_recv()
         up = ups[k] == 1
-        for pos in range(*groups[g]):
+        start, count = own(g)
+        for i in range(count):
+            pos = start + i
             got = s_recv[k, pos].astype(F32)
             if k < steps - 1:
                 mine = t_buf[pos]
@@ -158,9 +172,35 @@
                 new = rot(*table(2 * F + k), low) + high
                 t_buf[pos] = new
                 s_send[k + 1, pos] = new.astype(BF16)
-            r_buf[pos] = r_buf[pos] + rot(*table(2 * F + steps + k), got)
+            if k:
+                r_buf[pos] = r_buf[pos] + rot(*table(2 * F + steps + k), got)
         if k < steps - 1:
             hop(k + 1, g).start()
+
+    def swap(g, mine):
+        start, count = own(g)
+        if not mine:
+            start = groups[g][0] + (1 - core) * count
+        at = pl.ds(start, count)
+        return remote(c_send.at[at], c_recv.at[at], c_ssem.at[g], c_rsem.at[g],
+                      {"tm": partners[0]})
+
+    def share(g):
+        start, count = own(g)
+        for i in range(count):
+            c_send[start + i] = r_buf[start + i].astype(BF16)
+        swap(g, True).start()
+
+    def settle(g):
+        swap(g, False).wait_recv()
+        start, count = own(g)
+        for i in range(count):
+            pos = groups[g][0] + (1 - core) * count + i
+            r_buf[pos] = c_recv[pos].astype(F32)
+        for pos in range(*groups[g]):
+            r_buf[pos] = rot(*table(2 * F + steps), r_buf[pos]) + core.astype(F32) * s_recv[
+                0, pos
+            ].astype(F32)
 
     def states(g):
         for pos in range(*groups[g]):
@@ -181,8 +221,6 @@
     acc[0:1] = taps(x1, win, 0, 1, 1, 3)
     combine(0, 0)
     acc[R - 1:R] = taps(x1, win, R - 1, 1, 0, 2)
-    if steps > 1:
-        combine(1, 0)
     for s in range(2):
         @pl.when(sides[s][0])
         def _():
@@ -196,6 +234,7 @@
     acc[R - 1:R] += taps(x1, win, R - 1, 1, 2, 3)
     local_scan(1)
     hop(0, 1).start()
+    combine(1, 0)
 
     lh = [
         remote(lh_send.at[s], lh_recv.at[1 - s], lh_ssem.at[s], lh_rsem.at[1 - s],
@@ -207,10 +246,11 @@
         for s in range(2)
     ]
     ih = [
-        remote(ih_send.at[s], ih_recv.at[1 - s], ih_ssem.at[s], ih_rsem.at[1 - s],
-               {"row": sides[s][1]})
-        for s in range(2)
-    ]
+        remote(ih_send.at[j], ih_recv.at[1 - core], ih_ssem.at[j], ih_rsem.at[1 - core],
+               {"tm": chip + j, "row": row - 1 + 2 * core})
+        for j in range(2)
+    ]
+    ih_out = jnp.where(core == 0, row > 0, row < n_row - 1)
     ih_in = [
         remote(ih_send.at[s], ih_recv.at[s], ih_ssem.at[s], ih_rsem.at[s], {"row": sides[s][1]})
         for s in range(2)
@@ -222,25 +262,34 @@
         def _():
             lh[s].start()
 
+    combine(0, 1)
     for k in range(2, steps):
         combine(k, 0)
+    share(0)
+    combine(1, 1)
     ld_wout.wait()
+    settle(0)
     states(0)
     acc[1:2] = taps(x2, wout, 1, 1, 1, 3)
-    combine(0, 1)
+    for k in range(2, steps):
+        combine(k, 1)
+    pos = R - 2 + core
+    inc = r_buf[pos]
+    rate = [jnp.where(core == 0, a, b) for a, b in zip(table(2 * F - 1), table(2 * F + steps))]
+    early = jnp.where(core == 0, s_send[0, pos].astype(F32), s_recv[0, pos].astype(F32))
+    ih_send[0] = inc.astype(BF16)
+    ih_send[1] = (rot(*rate, inc) + early).astype(BF16)
+
+    @pl.when(ih_out)
+    def _():
+        for j in range(2):
+            ih[j].start()
+
+    share(1)
     acc[R - 2:R - 1] = taps(x2, wout, R - 2, 1, 0, 2)
-    if steps > 1:
-        combine(1, 1)
     acc[0:1] = taps(x2, wout, 0, 1, 2, 3)
     acc[R - 1:R] = taps(x2, wout, R - 1, 1, 0, 1)
-    for k in range(2, steps):
-        combine(k, 1)
-    for s in range(2):
-        ih_send[s] = r_buf[R - 2 + s].astype(BF16)
-
-        @pl.when(sides[s][0])
-        def _():
-            ih[s].start()
+    settle(1)
     states(1)
 
     def finish(r, v):
@@ -266,6 +315,13 @@
     finish(0, acc[0] + taps(x2, wout, 0, 1, 0, 1)[0])
     finish(R - 1, acc[R - 1] + taps(x2, wout, R - 1, 1, 2, 3)[0])
 
+    @pl.when(ih_out)
+    def _():
+        for j in range(2):
+            ih[j].wait_send()
+
+    for g in range(2):
+        swap(g, True).wait_send()
     for k in range(steps):
         for g in range(2):
             hop(k, g).wait_send()
@@ -274,7 +330,6 @@
         def _():
             fh[s].wait_send()
             lh[s].wait_send()
-            ih[s].wait_send()
 
 
 def solution(mesh):
@@ -284,7 +339,7 @@
 
     def shards(frames_in, state_in, modulus, angle, w_in, w_out):
         F, R, W, C = frames_in.shape
-        assert R >= 4
+        assert R == 4 and steps > 1
         n_table = -(-(2 * F + 2 * steps) // 8) * 8
         anywhere = pl.BlockSpec(memory_space=pl.ANY)
         vmem = pl.BlockSpec(memory_space=pltpu.VMEM)
@@ -315,9 +370,13 @@
                 pltpu.VMEM((2, FW, C), BF16),
                 pltpu.VMEM((2, W, C), BF16),
                 pltpu.VMEM((2, W, C), BF16),
+                pltpu.VMEM((R, W, C), BF16),
+                pltpu.VMEM((R, W, C), BF16),
                 dma((4,)),
                 dma((steps, 2)),
                 dma((steps, 2)),
+                dma((2,)),
+                dma((2,)),
                 dma((2,)),
                 dma((2,)),
                 dma((2,)),

time: 36.7 us -> 31.2 us (0.85)
  Pallas kernels: 34.2 us -> 28.6 us
    pallas_call x1, Pallas kernels: 34.2 us -> 28.6 us  [shards(): pl.pallas_call(functools.partial(kernel, n_tm, n_row, steps), out_shape=j...]
where the time goes in v2:
time: 31.2 us; the launch traced here: 30.9 us
  Pallas kernels  28.6 us (92%)
  local copies, waits for them, and re-layouts  2.29 us (7%)
    pallas_call x1, Pallas kernels, shards(): pl.pallas_call(functools.partial(kernel, n_tm, n_row, steps), out_shape=j...  28.6 us
    unnamed x1, local copies, waits for them, and re-layouts  2.29 us

profile of v2, /device:TPU:0, one launch (start us, length us, event | category | flops | bytes accessed | tf_op | source)
XLA Modules:
  0.0 30.9 jit_solution(4355651340987396640)
XLA Ops:
  0.0 28.6 %shard_map.64 = bf16[4,4,64,512]{3,2,1,0:T(8,128)(2,1)} custom-call(bf16[4,4,64,512]{3,2,1,0:T(8,128)(2,1)} %frames_hbm.1, f32[4,64,512]{2,1,0:T(8,128)} %state_hbm.1, f32[32,256]{1,0:T(8,128)} %mod_ref.1, f32[1,256]{1,0:T(1,128)} %bitcast.5, bf16[4608,512]{1,0:T(8,128)(2,1)} %bitcast.3, bf16[4608,512]{1,0:T(8,128)(2,1)} %bitcast.4), custom_call_target="tpu_custom_call" | custom-call | tf_op jit(solution)/shard_map/pallas_call | solution.py:348
  28.6 2.3 %copy.8 = bf16[4,4,64,512]{3,2,1,0:T(8,128)(2,1)} copy(bf16[4,4,64,512]{3,2,1,0:T(8,128)(2,1)} %shard_map.64) | data formatting | bytes 2097152
